TPU v7x, 32 devices: a whole 2x2x4 slice. The times are simulated.
32 devices in a mesh: dp: 4 (over y, core), cent: 8 (over z, x).
Axes of the slice: x: 2, y: 2, z: 4, core: 2. Of those that a mesh axis runs over, the one named last changes fastest.
Arguments:
- fragments: bfloat16 [8192, 1024], P(('dp', 'cent')), may hold values from -1500 to 1500
- order: int32 [32, 256], P(('dp', 'cent')), may hold values from 0 to 255, each once within a row
- group_ids: int32 [8192, 1], P(('dp', 'cent')), may hold values from 0 to 7; in each aligned block of 256 rows (0 to 255, 256 to 511, ...) at most 64 rows name the same one
- w_first: bfloat16 [1024, 1024], replicated, may hold values from -0.1875 to 0.1875
- w_second: bfloat16 [1024, 256], replicated, may hold values from -0.1875 to 0.1875
- centroids: float32 [8192, 256], P('cent'), may hold values from -24 to 24
Outputs:
- centroids_out: float32 [8192, 256], P('cent')
Inputs may be any that keep to these rules, and one draw needn't show every extreme that they name: `order`: each row is a permutation of 0 to 255. `group_ids`: among the rows of one device (aligned blocks of 256 rows) no group is named by more than 64 rows, a bound that some block reaches.
All inputs are finite; a program needn't handle non-finite values.
Results may differ from a plain program's by a relative error of at most 0.0075.
Values may be sent and summed in bfloat16 or wider, within the bound.
A program may use at most 64 MiB of HBM per device.

v0:
```python
import jax
import jax.numpy as jnp
from jax import lax
from jax.sharding import PartitionSpec as P

STEPS = 2
beta_scale = 0.0625
prior_weight = 1.0
eps_value = 1e-05


def per_device(fragments, order, group_ids, w_first, w_second, centroids):
    rows_here = fragments.shape[0]
    picked = jnp.take(fragments, order[0], axis=0)
    hidden = jax.nn.gelu(
        jnp.dot(picked, w_first, preferred_element_type=jnp.float32), approximate=True
    ).astype(jnp.bfloat16)
    proj = jnp.dot(hidden, w_second, preferred_element_type=jnp.float32)
    total_rows = float(rows_here * lax.axis_size("dp") * lax.axis_size("cent"))
    mean = lax.psum(jnp.sum(proj, axis=0), ("dp", "cent")) / total_rows
    var = lax.psum(jnp.sum((proj - mean) ** 2, axis=0), ("dp", "cent")) / total_rows
    zrows = ((proj - mean) * lax.rsqrt(var + eps_value)).astype(jnp.bfloat16)
    width = zrows.shape[1]
    groups = group_ids[:, 0]
    group_count = lax.axis_size("cent")
    capacity = 2 * rows_here // group_count
    member = (groups[:, None] == jnp.arange(group_count, dtype=jnp.int32)[None, :]).astype(
        jnp.float32
    )
    index = jnp.arange(rows_here, dtype=jnp.int32)
    before = (index[:, None] > index[None, :]).astype(jnp.float32)
    rank = jnp.sum(jnp.dot(before, member) * member, axis=1).astype(jnp.int32)
    slot = groups * capacity + rank
    place = (slot[:, None] == jnp.arange(group_count * capacity, dtype=jnp.int32)[None, :]).astype(
        jnp.bfloat16
    )
    packed = lax.dot_general(
        place, zrows, (((0,), (0,)), ((), ())), preferred_element_type=jnp.float32
    ).astype(jnp.bfloat16)
    filled = jnp.sum(place.astype(jnp.float32), axis=0).astype(jnp.bfloat16)
    received, live = (
        lax.all_to_all(
            packed.reshape(group_count, capacity, width),
            "cent",
            split_axis=0,
            concat_axis=0,
            tiled=True,
        ),
        lax.all_to_all(
            filled.reshape(group_count, capacity), "cent", split_axis=0, concat_axis=0, tiled=True
        ),
    )
    received = received.reshape(group_count * capacity, width)
    live_rows = live.reshape(group_count * capacity).astype(jnp.float32)
    current = centroids
    parts_dp = lax.axis_size("dp")
    where_dp = lax.axis_index("dp")
    for step in range(STEPS):
        rounded = current.astype(jnp.bfloat16)
        cnorm = jnp.sum(current * current, axis=1)
        cross = lax.dot_general(
            received, rounded, (((1,), (1,)), ((), ())), preferred_element_type=jnp.float32
        )
        scores = beta_scale * (2.0 * cross - cnorm[None, :])
        top = jnp.max(scores, axis=1, keepdims=True)
        expo = jnp.exp(scores - top)
        resp = (expo / jnp.sum(expo, axis=1, keepdims=True) * live_rows[:, None]).astype(
            jnp.bfloat16
        )
        num = lax.dot_general(
            resp, received, (((0,), (0,)), ((), ())), preferred_element_type=jnp.float32
        )
        den = jnp.sum(resp.astype(jnp.float32), axis=0)
        share = current.shape[0] // parts_dp
        num_part, den_part = (
            lax.psum_scatter(num, "dp", scatter_dimension=0, tiled=True),
            lax.psum_scatter(den, "dp", scatter_dimension=0, tiled=True),
        )
        old = lax.dynamic_slice_in_dim(current, where_dp * share, share, 0)
        fresh = (num_part + prior_weight * old) / (den_part + prior_weight)[:, None]
        current = lax.all_gather(fresh, "dp", axis=0, tiled=True)
    return current


def solution(mesh):
    return jax.shard_map(
        per_device,
        mesh=mesh,
        in_specs=(
            P(("dp", "cent"), None),
            P(("dp", "cent"), None),
            P(("dp", "cent"), None),
            P(),
            P(),
            P("cent", None),
        ),
        out_specs=P("cent", None),
        check_vma=False,
    )
```

profile of v0, /device:TPU:0, one launch (start us, length us, event | category | flops | bytes accessed | tf_op | source)
XLA Modules:
  0.0 222.9 jit_solution(5794457838258072373)
XLA Ops:
  6.5 1.0 fusion.2
  7.6 0.7 multiply_add_fusion
  9.1 7.3 %all-to-all-start.1 = ((bf16[8,1,64]{2,1,0:T(2,128)(2,1)}), bf16[8,1,64]{2,1,0:T(2,128)(2,1)S(1)}, u32[]{:S(2)}, u32[]{:S(2)}) async-start(bf16[8,1,64]{2,1,0:T(2,128)(2,1)} %all_to_all.12), calls=%async_computation.1 | async-start | bytes 8192 | tf_op jit(solution)/shard_map/all_to_all | solution.py:49
  17.0 0.7 compare_and_fusion
  17.7 3.5 %gather_fusion = bf16[256,1024]{1,0:T(8,128)(2,1)} fusion(bf16[256,1024]{1,0:T(8,128)(2,1)} %param.6, s32[1024]{0:T(1024)S(1)} %pad_clamp_fusion), kind=kCustom, calls=%fused_computation | custom fusion | bytes 1049600 | tf_op jit(solution)/shard_map/jit(_take)/gather | solution.py:14
  21.2 2.4 %fusion.36 = (f32[256]{0:T(256)S(1)}, f32[256,256]{1,0:T(8,128)S(1)}) fusion(bf16[1024,256]{1,0:T(8,128)(2,1)} %param.10, bf16[1024,1024]{1,0:T(8,128)(2,1)S(1)} %copy-done, bf16[256,1024]{1,0:T(8,128)(2,1)} %gather_fusion, pred[256]{0:T(512)(128)(4,1)S(1)} %compare_and_fusion), kind=kOutput, calls=%fused_computation.60 | convolution fusion | flops 673775360 | bytes 3409152 | tf_op jit(solution)/shard_map/dot_general | solution.py:18
  23.6 40.8 %psum.14 = f32[256]{0:T(256)S(1)} all-reduce(f32[256]{0:T(256)S(1)} %get-tuple-element.9), channel_id=1, replica_groups=mesh['dp'=4,'cent'=8] {'dp','cent'}, use_global_device_ids=true, to_apply=%region_2.3 | all-reduce | flops 256 | bytes 2048 | tf_op jit(solution)/shard_map/psum | solution.py:20
  64.5 40.0 %psum.15 = f32[256]{0:T(256)S(1)} all-reduce(f32[256]{0:T(256)S(1)} %multiply_reduce_fusion.2), channel_id=1, replica_groups=mesh['dp'=4,'cent'=8] {'dp','cent'}, use_global_device_ids=true, to_apply=%region_4.5 | all-reduce | flops 256 | bytes 2048 | tf_op jit(solution)/shard_map/psum | solution.py:21
  104.6 1.1 convolution_convert_fusion
  105.7 5.3 %all-to-all-start = ((bf16[8,64,256]{2,1,0:T(8,128)(2,1)}), bf16[8,64,256]{2,1,0:T(8,128)(2,1)S(1)}, u32[]{:S(2)}, u32[]{:S(2)}) async-start(bf16[8,64,256]{2,1,0:T(8,128)(2,1)} %bitcast.22), calls=%async_computation | async-start | bytes 524288 | tf_op jit(solution)/shard_map/all_to_all | solution.py:42
  111.4 7.9 %all-to-all-done = bf16[8,64,256]{2,1,0:T(8,128)(2,1)S(1)} async-done(((bf16[8,64,256]{2,1,0:T(8,128)(2,1)}), bf16[8,64,256]{2,1,0:T(8,128)(2,1)S(1)}, u32[]{:S(2)}, u32[]{:S(2)}) %all-to-all-start) | async-done | bytes 262176 | tf_op jit(solution)/shard_map/all_to_all | solution.py:42
  121.0 1.5 fusion.41
  123.8 5.7 %all-reduce = f32[1024]{0:T(1024)S(1)} all-reduce(f32[1024]{0:T(1024)S(1)} %get-tuple-element.7), channel_id=3, replica_groups=mesh['dp'=4,'cent'=8] {'dp'}, use_global_device_ids=true, to_apply=%region_11.12.clone | all-reduce | flops 1024 | bytes 8192
  129.6 16.2 %reduce-scatter.3.cloned.1.call-done = f32[256,256]{1,0:T(8,128)} async-done(((f32[1024,256]{1,0:T(8,128)}), f32[256,256]{1,0:T(8,128)}) %reduce-scatter.3.cloned.1.call-update) | async-done | bytes 262160 | tf_op jit(solution)/shard_map/reduce_scatter | solution.py:76
  145.8 1.8 add_divide_fusion.1
  147.6 16.8 %all-gather.3.cloned.1.call-done = f32[1024,256]{1,0:T(8,128)} async-done(((f32[256,256]{1,0:T(8,128)}), f32[1024,256]{1,0:T(8,128)}) %all-gather.3.cloned.1.call-update) | async-done | bytes 1048592 | tf_op jit(solution)/shard_map/all_gather | solution.py:81
  164.5 1.4 multiply_reduce_fusion
  165.9 1.8 fusion.40
  168.9 1.5 fusion.42
  170.4 5.9 %all-reduce.1 = f32[1024]{0:T(1024)S(1)} all-reduce(f32[1024]{0:T(1024)S(1)} %get-tuple-element.5), channel_id=5, replica_groups=mesh['dp'=4,'cent'=8] {'dp'}, use_global_device_ids=true, to_apply=%region_17.18.clone | all-reduce | flops 1024 | bytes 8192
  176.4 19.0 %reduce-scatter.5.cloned.1.call-done = f32[256,256]{1,0:T(8,128)} async-done(((f32[1024,256]{1,0:T(8,128)}), f32[256,256]{1,0:T(8,128)}) %reduce-scatter.5.cloned.1.call-update) | async-done | bytes 262160 | tf_op jit(solution)/shard_map/reduce_scatter | solution.py:76
  195.4 1.8 add_divide_fusion
  197.3 16.9 %all-gather.5.cloned.1.call-done = f32[1024,256]{1,0:T(8,128)} async-done(((f32[256,256]{1,0:T(8,128)}), f32[1024,256]{1,0:T(8,128)}) %all-gather.5.cloned.1.call-update) | async-done | bytes 1048592 | tf_op jit(solution)/shard_map/all_gather | solution.py:81
  214.1 2.3 %copy.10 = f32[1024,256]{1,0:T(8,128)} copy(f32[1024,256]{1,0:T(8,128)} %all-gather.5.cloned.1.call-done) | data formatting | bytes 2097152
  (34 shorter events, 5.8 us)
Async XLA Ops:
  6.5 14.7 %copy-start = (bf16[1024,1024]{1,0:T(8,128)(2,1)S(1)}, bf16[1024,1024]{1,0:T(8,128)(2,1)}, u32[]{:S(2)}) copy-start(bf16[1024,1024]{1,0:T(8,128)(2,1)} %param.9) | copy-start | bytes 6291460
  9.1 96.6 %all-to-all-start.1 = ((bf16[8,1,64]{2,1,0:T(2,128)(2,1)}), bf16[8,1,64]{2,1,0:T(2,128)(2,1)S(1)}, u32[]{:S(2)}, u32[]{:S(2)}) async-start(bf16[8,1,64]{2,1,0:T(2,128)(2,1)} %all_to_all.12), calls=%async_computation.1 | async-start | bytes 8192 | tf_op jit(solution)/shard_map/all_to_all | solution.py:49
  21.2 89.9 %copy-start.1 = (f32[1024,256]{1,0:T(8,128)S(1)}, f32[1024,256]{1,0:T(8,128)}, u32[]{:S(2)}) copy-start(f32[1024,256]{1,0:T(8,128)} %param.11) | copy-start | bytes 3145732
  105.7 13.6 %all-to-all-start = ((bf16[8,64,256]{2,1,0:T(8,128)(2,1)}), bf16[8,64,256]{2,1,0:T(8,128)(2,1)S(1)}, u32[]{:S(2)}, u32[]{:S(2)}) async-start(bf16[8,64,256]{2,1,0:T(8,128)(2,1)} %bitcast.22), calls=%async_computation | async-start | bytes 524288 | tf_op jit(solution)/shard_map/all_to_all | solution.py:42
  111.0 34.8 %reduce-scatter.3.cloned.1.call-start = ((), (), s32[]{:S(2)}) async-start(), calls=%async_computation.4 | async-start | bytes 1310720 | tf_op jit(solution)/shard_map/reduce_scatter | solution.py:76
  121.0 1.5 copy-start.2
  122.5 42.0 %all-gather.3.cloned.1.call-start = ((), (), s32[]{:S(2)}) async-start(), calls=%async_computation.5 | async-start | bytes 1310720 | tf_op jit(solution)/shard_map/all_gather | solution.py:81
  147.6 47.8 %reduce-scatter.5.cloned.1.call-start = ((), (), s32[]{:S(2)}) async-start(), calls=%async_computation.6 | async-start | bytes 1310720 | tf_op jit(solution)/shard_map/reduce_scatter | solution.py:76
  170.3 43.8 %all-gather.5.cloned.1.call-start = ((), (), s32[]{:S(2)}) async-start(), calls=%async_computation.7 | async-start | bytes 1310720 | tf_op jit(solution)/shard_map/all_gather | solution.py:81
Sparse Core Ops, SparseCore 0:
  122.6 23.1 reduce-scatter.2
  147.7 16.7 all-gather.2
  170.5 24.8 reduce-scatter.4
  197.4 16.7 all-gather.4
where the time goes:
time: 224 us; the launch traced here: 223 us
  blocking collectives  92.4 us (41%)
  waiting for transfers between devices  77 us (34%)
  between operations  13.9 us (6%)
  starting transfers between devices  12.7 us (6%)
  other arithmetic  9.96 us (4%)
  matrix products  9.85 us (4%)
  local copies, waits for them, and re-layouts  7.14 us (3%)
    psum x1, blocking collectives, per_device(): mean = lax.psum(jnp.sum(proj, axis=0), ('dp', 'cent')) / total_rows  40.8 us
    psum x1, blocking collectives, per_device(): lax.psum(jnp.sum((proj - mean) ** 2, axis=0), ('dp', 'cent')) / total_rows  40 us
    reduce_scatter x2, waiting for transfers between devices, per_device(): lax.psum_scatter(num, 'dp', scatter_dimension=0, tiled=True)  35.3 us
    all_gather x2, waiting for transfers between devices, per_device(): current = lax.all_gather(fresh, 'dp', axis=0, tiled=True)  33.7 us
    unnamed x2, blocking collectives  11.6 us
    all_to_all x1, waiting for transfers between devices, per_device(): lax.all_to_all(packed.reshape(group_count, capacity, width), 'cent', spli...  7.92 us
    all_to_all x1, starting transfers between devices, per_device(): lax.all_to_all(filled.reshape(group_count, capacity), 'cent', split_axis=...  7.25 us
    all_to_all x1, starting transfers between devices, per_device(): lax.all_to_all(packed.reshape(group_count, capacity, width), 'cent', spli...  5.31 us
  transfers between devices with their start and end apart: 6, of which 5 were waited for; matrix products, arithmetic and copies ran while one was open for 4% of the time, Pallas kernels for 0%

commit v1 on v0

--- a/solution.py
+++ b/solution.py
@@ -78,7 +78,34 @@
         )
         old = lax.dynamic_slice_in_dim(current, where_dp * share, share, 0)
         fresh = (num_part + prior_weight * old) / (den_part + prior_weight)[:, None]
-        current = lax.all_gather(fresh, "dp", axis=0, tiled=True)
+
+        def supply_all_screen(axis_no, x0, which_axis):
+            mat_out, local_out, z1 = (
+                lax.psum(1, which_axis),
+                lax.axis_index(which_axis),
+                x0.shape[axis_no],
+            )
+            row_list = [(kk, (kk + 1) % mat_out) for kk in range(mat_out)]
+            panels = [(kk, (kk - 1) % mat_out) for kk in range(mat_out)]
+            u_next = jnp.zeros(
+                (*x0.shape[:axis_no], mat_out * z1, *x0.shape[axis_no + 1 :]), x0.dtype
+            )
+            u_next = lax.dynamic_update_slice_in_dim(u_next, x0, local_out * z1, axis=axis_no)
+            front = block_next = x0
+            block_now = mat_out // 2
+            for j in range(1, block_now + 1):
+                front = lax.ppermute(front, which_axis, row_list)
+                u_next = lax.dynamic_update_slice_in_dim(
+                    u_next, front, (local_out - j) % mat_out * z1, axis=axis_no
+                )
+                if j < mat_out - block_now:
+                    block_next = lax.ppermute(block_next, which_axis, panels)
+                    u_next = lax.dynamic_update_slice_in_dim(
+                        u_next, block_next, (local_out + j) % mat_out * z1, axis=axis_no
+                    )
+            return u_next
+
+        current = supply_all_screen(0, fresh, "dp")
     return current
 
 

time: 224 us -> 215 us (0.960)
  waiting for transfers between devices: 77 us -> 65.9 us
  starting transfers between devices: 12.7 us -> 16.2 us
    all_gather x2 -> x0, waiting for transfers between devices: 33.7 us -> none  [per_device(): current = lax.all_gather(fresh, 'dp', axis=0, tiled=True)]
    ppermute x0 -> x6, waiting for transfers between devices: none -> 22.8 us  [the longest x4 22.8 us: supply_all_screen(): front = lax.ppermute(front, which_axis, row_list)]
    dynamic_update_slice x0 -> x6, local copies, waits for them, and re-layouts: none -> 3.68 us  [the longest x4 2.68 us: supply_all_screen(): lax.dynamic_update_slice_in_dim(u_next, front, (local_out - j) % mat_out...]
    div x2 -> x0, other arithmetic: 3.6 us -> none  [per_device(): fresh = (num_part + prior_weight * old) / (den_part + prior_weight)[:, None]]
    ppermute x0 -> x6, starting transfers between devices: none -> 3.54 us  [the longest x2 3.48 us: supply_all_screen(): block_next = lax.ppermute(block_next, which_axis, panels)]
    dynamic_update_slice x0 -> x2, other arithmetic: none -> 2.91 us  [supply_all_screen(): lax.dynamic_update_slice_in_dim(u_next, x0, local_out * z1, axis=axis_no)]
    unnamed x8 -> x9, local copies, waits for them, and re-layouts: 2.92 us -> 0.67 us
  transfers between devices with their start and end apart: 6 -> 10, of which waited for: 5 -> 7; matrix products, arithmetic and copies ran while one was open for 4% -> 5% of each run, Pallas kernels for 0% -> 0%
where the time goes in v1:
time: 215 us; the launch traced here: 214 us
  blocking collectives  92.3 us (43%)
  waiting for transfers between devices  65.9 us (31%)
  starting transfers between devices  16.2 us (8%)
  between operations  14.2 us (7%)
  local copies, waits for them, and re-layouts  8.7 us (4%)
  matrix products  8.63 us (4%)
  other arithmetic  8.27 us (4%)
    psum x1, blocking collectives, per_device(): mean = lax.psum(jnp.sum(proj, axis=0), ('dp', 'cent')) / total_rows  40.8 us
    psum x1, blocking collectives, per_device(): lax.psum(jnp.sum((proj - mean) ** 2, axis=0), ('dp', 'cent')) / total_rows  40.1 us
    reduce_scatter x2, waiting for transfers between devices, per_device(): lax.psum_scatter(num, 'dp', scatter_dimension=0, tiled=True)  35.1 us
    ppermute x4, waiting for transfers between devices, supply_all_screen(): front = lax.ppermute(front, which_axis, row_list)  22.8 us
    unnamed x2, blocking collectives  11.4 us
    all_to_all x1, waiting for transfers between devices, per_device(): lax.all_to_all(packed.reshape(group_count, capacity, width), 'cent', spli...  7.94 us
    all_to_all x1, starting transfers between devices, per_device(): lax.all_to_all(filled.reshape(group_count, capacity), 'cent', split_axis=...  7.25 us
    all_to_all x1, starting transfers between devices, per_device(): lax.all_to_all(packed.reshape(group_count, capacity, width), 'cent', spli...  5.31 us
  transfers between devices with their start and end apart: 10, of which 7 were waited for; matrix products, arithmetic and copies ran while one was open for 5% of the time, Pallas kernels for 0%

profile of v1, /device:TPU:0, one launch (start us, length us, event | category | flops | bytes accessed | tf_op | source)
XLA Modules:
  0.0 214.2 jit_solution(12631644457723875089)
XLA Ops:
  6.5 1.0 fusion.3
  9.1 7.3 %all-to-all-start.1 = ((bf16[8,1,64]{2,1,0:T(2,128)(2,1)}), bf16[8,1,64]{2,1,0:T(2,128)(2,1)S(1)}, u32[]{:S(2)}, u32[]{:S(2)}) async-start(bf16[8,1,64]{2,1,0:T(2,128)(2,1)} %all_to_all.12), calls=%async_computation.1 | async-start | bytes 8192 | tf_op jit(solution)/shard_map/all_to_all | solution.py:49
  17.7 3.5 %gather_fusion = bf16[256,1024]{1,0:T(8,128)(2,1)} fusion(bf16[256,1024]{1,0:T(8,128)(2,1)} %param.6, s32[1024]{0:T(1024)S(1)} %pad_clamp_fusion), kind=kCustom, calls=%fused_computation | custom fusion | bytes 1049600 | tf_op jit(solution)/shard_map/jit(_take)/gather | solution.py:14
  21.2 2.4 %fusion.38 = (f32[256]{0:T(256)S(1)}, f32[256,256]{1,0:T(8,128)S(1)}) fusion(bf16[1024,256]{1,0:T(8,128)(2,1)} %param.10, bf16[1024,1024]{1,0:T(8,128)(2,1)S(1)} %copy-done, bf16[256,1024]{1,0:T(8,128)(2,1)} %gather_fusion, pred[256]{0:T(512)(128)(4,1)S(1)} %compare_and_fusion), kind=kOutput, calls=%fused_computation.70 | convolution fusion | flops 673775360 | bytes 3409152 | tf_op jit(solution)/shard_map/dot_general | solution.py:18
  23.6 40.8 %psum.14 = f32[256]{0:T(256)S(1)} all-reduce(f32[256]{0:T(256)S(1)} %get-tuple-element.13), channel_id=1, replica_groups=mesh['dp'=4,'cent'=8] {'dp','cent'}, use_global_device_ids=true, to_apply=%region_2.3 | all-reduce | flops 256 | bytes 2048 | tf_op jit(solution)/shard_map/psum | solution.py:20
  64.5 40.1 %psum.15 = f32[256]{0:T(256)S(1)} all-reduce(f32[256]{0:T(256)S(1)} %multiply_reduce_fusion.2), channel_id=1, replica_groups=mesh['dp'=4,'cent'=8] {'dp','cent'}, use_global_device_ids=true, to_apply=%region_4.5 | all-reduce | flops 256 | bytes 2048 | tf_op jit(solution)/shard_map/psum | solution.py:21
  104.6 1.1 convolution_convert_fusion
  105.7 5.3 %all-to-all-start = ((bf16[8,64,256]{2,1,0:T(8,128)(2,1)}), bf16[8,64,256]{2,1,0:T(8,128)(2,1)S(1)}, u32[]{:S(2)}, u32[]{:S(2)}) async-start(bf16[8,64,256]{2,1,0:T(8,128)(2,1)} %bitcast.22), calls=%async_computation | async-start | bytes 524288 | tf_op jit(solution)/shard_map/all_to_all | solution.py:42
  111.4 7.9 %all-to-all-done = bf16[8,64,256]{2,1,0:T(8,128)(2,1)S(1)} async-done(((bf16[8,64,256]{2,1,0:T(8,128)(2,1)}), bf16[8,64,256]{2,1,0:T(8,128)(2,1)S(1)}, u32[]{:S(2)}, u32[]{:S(2)}) %all-to-all-start) | async-done | bytes 262176 | tf_op jit(solution)/shard_map/all_to_all | solution.py:42
  121.0 1.5 fusion.42
  123.9 5.7 %all-reduce = f32[1024]{0:T(1024)S(1)} all-reduce(f32[1024]{0:T(1024)S(1)} %get-tuple-element.11), channel_id=3, replica_groups=mesh['dp'=4,'cent'=8] {'dp'}, use_global_device_ids=true, to_apply=%region_11.12.clone | all-reduce | flops 1024 | bytes 8192
  129.6 16.2 %reduce-scatter.3.cloned.1.call-done = f32[256,256]{1,0:T(8,128)} async-done(((f32[1024,256]{1,0:T(8,128)}), f32[256,256]{1,0:T(8,128)}) %reduce-scatter.3.cloned.1.call-update) | async-done | bytes 262160 | tf_op jit(solution)/shard_map/reduce_scatter | solution.py:76
  145.9 1.8 constant_dynamic-update-slice_fusion.7
  147.7 1.7 collective-permute-start.1
  149.5 6.6 %collective-permute-done = f32[256,256]{1,0:T(8,128)} collective-permute-done((f32[256,256]{1,0:T(8,128)}, f32[256,256]{1,0:T(8,128)}, u32[]{:S(2)}, u32[]{:S(2)}) %collective-permute-start) | collective-permute-done | bytes 262176 | tf_op jit(solution)/shard_map/ppermute | solution.py:97
  157.1 1.0 constant_dynamic-update-slice_fusion.5
  158.0 4.2 %collective-permute-done.2 = f32[256,256]{1,0:T(8,128)} collective-permute-done((f32[256,256]{1,0:T(8,128)}, f32[256,256]{1,0:T(8,128)}, u32[]{:S(2)}, u32[]{:S(2)}) %collective-permute-start.2) | collective-permute-done | bytes 262176 | tf_op jit(solution)/shard_map/ppermute | solution.py:97
  165.3 1.5 fusion.43
  166.8 5.8 %all-reduce.1 = f32[1024]{0:T(1024)S(1)} all-reduce(f32[1024]{0:T(1024)S(1)} %get-tuple-element.7), channel_id=5, replica_groups=mesh['dp'=4,'cent'=8] {'dp'}, use_global_device_ids=true, to_apply=%region_17.18.clone | all-reduce | flops 1024 | bytes 8192
  172.6 18.9 %reduce-scatter.5.cloned.1.call-done = f32[256,256]{1,0:T(8,128)} async-done(((f32[1024,256]{1,0:T(8,128)}), f32[256,256]{1,0:T(8,128)}) %reduce-scatter.5.cloned.1.call-update) | async-done | bytes 262160 | tf_op jit(solution)/shard_map/reduce_scatter | solution.py:76
  191.6 1.1 constant_dynamic-update-slice_fusion.3
  192.8 1.7 collective-permute-start.4
  194.5 6.3 %collective-permute-done.3 = f32[256,256]{1,0:T(8,128)S(1)} collective-permute-done((f32[256,256]{1,0:T(8,128)S(1)}, f32[256,256]{1,0:T(8,128)S(1)}, u32[]{:S(2)}, u32[]{:S(2)}) %collective-permute-start.3) | collective-permute-done | bytes 262176 | tf_op jit(solution)/shard_map/ppermute | solution.py:97
  200.9 5.7 %collective-permute-done.5 = f32[256,256]{1,0:T(8,128)S(1)} collective-permute-done((f32[256,256]{1,0:T(8,128)S(1)}, f32[256,256]{1,0:T(8,128)S(1)}, u32[]{:S(2)}, u32[]{:S(2)}) %collective-permute-start.5) | collective-permute-done | bytes 262176 | tf_op jit(solution)/shard_map/ppermute | solution.py:97
  (49 shorter events, 10.9 us)
Async XLA Ops:
  6.5 14.6 %copy-start = (bf16[1024,1024]{1,0:T(8,128)(2,1)S(1)}, bf16[1024,1024]{1,0:T(8,128)(2,1)}, u32[]{:S(2)}) copy-start(bf16[1024,1024]{1,0:T(8,128)(2,1)} %param.9) | copy-start | bytes 6291460
  9.1 96.6 %all-to-all-start.1 = ((bf16[8,1,64]{2,1,0:T(2,128)(2,1)}), bf16[8,1,64]{2,1,0:T(2,128)(2,1)S(1)}, u32[]{:S(2)}, u32[]{:S(2)}) async-start(bf16[8,1,64]{2,1,0:T(2,128)(2,1)} %all_to_all.12), calls=%async_computation.1 | async-start | bytes 8192 | tf_op jit(solution)/shard_map/all_to_all | solution.py:49
  21.2 89.9 %copy-start.1 = (f32[1024,256]{1,0:T(8,128)S(1)}, f32[1024,256]{1,0:T(8,128)}, u32[]{:S(2)}) copy-start(f32[1024,256]{1,0:T(8,128)} %param.11) | copy-start | bytes 3145732
  105.7 13.6 %all-to-all-start = ((bf16[8,64,256]{2,1,0:T(8,128)(2,1)}), bf16[8,64,256]{2,1,0:T(8,128)(2,1)S(1)}, u32[]{:S(2)}, u32[]{:S(2)}) async-start(bf16[8,64,256]{2,1,0:T(8,128)(2,1)} %bitcast.22), calls=%async_computation | async-start | bytes 524288 | tf_op jit(solution)/shard_map/all_to_all | solution.py:42
  111.0 34.8 %reduce-scatter.3.cloned.1.call-start = ((), (), s32[]{:S(2)}) async-start(), calls=%async_computation.4 | async-start | bytes 1310720 | tf_op jit(solution)/shard_map/reduce_scatter | solution.py:76
  121.0 1.5 copy-start.3
  122.5 69.0 %reduce-scatter.5.cloned.1.call-start = ((), (), s32[]{:S(2)}) async-start(), calls=%async_computation.5 | async-start | bytes 1310720 | tf_op jit(solution)/shard_map/reduce_scatter | solution.py:76
  147.7 8.3 %collective-permute-start = (f32[256,256]{1,0:T(8,128)}, f32[256,256]{1,0:T(8,128)}, u32[]{:S(2)}, u32[]{:S(2)}) collective-permute-start(f32[256,256]{1,0:T(8,128)} %get-tuple-element.10), channel_id=1, source_target_pairs={{0,8},{8,16},{16,24},{24,0},{1,9},{9,17},{17,25},{25,1},{2,10},{10... | collective-permute-start | bytes 786440 | tf_op jit(solution)/shard_map/ppermute | solution.py:97
  147.7 9.3 %collective-permute-start.1 = (f32[256,256]{1,0:T(8,128)}, f32[256,256]{1,0:T(8,128)}, u32[]{:S(2)}, u32[]{:S(2)}) collective-permute-start(f32[256,256]{1,0:T(8,128)} %get-tuple-element.10), channel_id=1, source_target_pairs={{0,24},{8,0},{16,8},{24,16},{1,25},{9,1},{17,9},{25,17},{2,26},{10... | collective-permute-start | bytes 786440 | tf_op jit(solution)/shard_map/ppermute | solution.py:102
  156.1 6.1 %collective-permute-start.2 = (f32[256,256]{1,0:T(8,128)}, f32[256,256]{1,0:T(8,128)}, u32[]{:S(2)}, u32[]{:S(2)}) collective-permute-start(f32[256,256]{1,0:T(8,128)} %collective-permute-done), channel_id=1, source_target_pairs={{0,8},{8,16},{16,24},{24,0},{1,9},{9,17},{17,25},{25,1},{2,10},{10... | collective-permute-start | bytes 786440 | tf_op jit(solution)/shard_map/ppermute | solution.py:97
  192.7 8.1 %collective-permute-start.3 = (f32[256,256]{1,0:T(8,128)S(1)}, f32[256,256]{1,0:T(8,128)S(1)}, u32[]{:S(2)}, u32[]{:S(2)}) collective-permute-start(f32[256,256]{1,0:T(8,128)S(1)} %get-tuple-element.6), channel_id=1, source_target_pairs={{0,8},{8,16},{16,24},{24,0},{1,9},{9,17},{17,25},{25,1},{2,10},{10... | collective-permute-start | bytes 786440 | tf_op jit(solution)/shard_map/ppermute | solution.py:97
  192.8 8.1 %collective-permute-start.4 = (f32[256,256]{1,0:T(8,128)S(1)}, f32[256,256]{1,0:T(8,128)S(1)}, u32[]{:S(2)}, u32[]{:S(2)}) collective-permute-start(f32[256,256]{1,0:T(8,128)S(1)} %get-tuple-element.6), channel_id=1, source_target_pairs={{0,24},{8,0},{16,8},{24,16},{1,25},{9,1},{17,9},{25,17},{2,26},{10... | collective-permute-start | bytes 786440 | tf_op jit(solution)/shard_map/ppermute | solution.py:102
  200.8 5.8 %collective-permute-start.5 = (f32[256,256]{1,0:T(8,128)S(1)}, f32[256,256]{1,0:T(8,128)S(1)}, u32[]{:S(2)}, u32[]{:S(2)}) collective-permute-start(f32[256,256]{1,0:T(8,128)S(1)} %collective-permute-done.3), channel_id=1, source_target_pairs={{0,8},{8,16},{16,24},{24,0},{1,9},{9,17},{17,25},{25,1},{2,10},{10... | collective-permute-start | bytes 786440 | tf_op jit(solution)/shard_map/ppermute | solution.py:97
  200.9 5.7 %copy-start.2 = (f32[1024,256]{1,0:T(8,128)}, f32[1024,256]{1,0:T(8,128)S(1)}, u32[]{:S(2)}) copy-start(f32[1024,256]{1,0:T(8,128)S(1)} %constant_dynamic-update-slice_fusion.1) | copy-start | bytes 3145732
Sparse Core Ops, SparseCore 0:
  122.6 23.1 reduce-scatter.2
  166.9 24.6 reduce-scatter.4
